TPU v7x, 256 devices: a whole 4x4x8 slice. The times are simulated.
256 devices in a mesh: ens: 4 (over y), band: 64 (over z, x, core).
Axes of the slice: x: 4, y: 4, z: 8, core: 2. Of those that a mesh axis runs over, the one named last changes fastest.
Arguments:
- spectral_state: bfloat16 [1536, 384, 256], P(('ens', 'band')), parts along dimension 0, may hold values from -0.29882812 to 0.29882812
- lat_basis: bfloat16 [384, 640, 384], P('band'), may hold values from -0.3125 to 0.3125
- quad_weight: float32 [640], P('band'), may hold values from 0.5 to 2
- wave_of_slot: int32 [384], replicated, may hold values from 0 to 383, each once
- dest_owner: int32 [640, 1440], P('band'), may hold values from 0 to 63, as said below
- dest_slot: int32 [640, 1440], P('band'), may hold values from 0 to 14399, as said below
- surface: bfloat16 [921600, 128], P('band'), may hold values from -6 to 6
- in_weight: bfloat16 [128, 256], replicated, may hold values from -0.5 to 0.5
- surface_weight: bfloat16 [128, 256], replicated, may hold values from -0.5 to 0.5
- in_bias: float32 [256], replicated, may hold values from -3 to 3
- mid_weight: bfloat16 [256, 256], replicated, may hold values from -0.375 to 0.375
- mid_bias: float32 [256], replicated, may hold values from -3 to 3
- out_weight: bfloat16 [256, 128], replicated, may hold values from -0.375 to 0.375
Outputs:
- spectral_tendency: float32 [1536, 384, 256], P(('ens', 'band')), parts along dimension 0
There are 4 independent parts, one for each index of `ens`. A program takes and returns all parts, laid end to end along the dimension named above; an argument that names none is the same for every part. Nothing has to cross between parts.
Inputs may be any that keep to these rules, and one draw needn't show every extreme that they name: `wave_of_slot`: each number once. `dest_owner`: the columns of each band of 10 latitudes are dealt in turn to the owners along a Hilbert curve over the grid; every band gives exactly 225 columns to each owner. `dest_slot`: each owner's 14400 columns have different slots.
All inputs are finite; a program needn't handle non-finite values.
Results may differ from a plain program's by a relative error of at most 0.009.
Values may be sent and summed in bfloat16 or wider, within the bound.
No kernel may reach another device: no remote copies, remote signals or barrier semaphores. Data moves between devices by JAX's collectives and lax.ppermute only.
A program may use at most 128 MiB of HBM per device.

v0:
```python
import functools
import math

import jax
import jax.numpy as jnp
from jax import lax
from jax.experimental import pallas as pl
from jax.experimental.pallas import tpu as pltpu
from jax.sharding import PartitionSpec as P

VMEM_BYTES = 24 * 1024 * 1024


def whole(shape):
    zeros = (0,) * len(shape)
    return pl.BlockSpec(shape, lambda *_: zeros)


def fourier_kernel(basis_ref, state_ref, out_ref, wide):
    slots, lats, features = pl.num_programs(0), basis_ref.shape[1], out_ref.shape[1]
    slot = pl.program_id(0)
    per_lat = out_ref.shape[0] // lats
    found = jnp.dot(basis_ref[0], state_ref[0], preferred_element_type=jnp.float32)
    for k in range(2):
        wide[pl.ds(2 * slot + k, lats, per_lat), :] = found[:, k * features : (k + 1) * features]

    @pl.when(slot == slots - 1)
    def _():
        out_ref[...] = wide[...].astype(out_ref.dtype)


def to_latitudes(lat_basis, spectral_state):
    slots, lats, degrees = lat_basis.shape
    features = spectral_state.shape[2] // 2
    rows = lats * slots * 2
    return pl.pallas_call(
        fourier_kernel,
        grid=(slots,),
        in_specs=[
            pl.BlockSpec((1, lats, degrees), lambda s: (s, 0, 0)),
            pl.BlockSpec((1, degrees, 2 * features), lambda s: (s, 0, 0)),
        ],
        out_specs=whole((rows, features)),
        out_shape=jax.ShapeDtypeStruct((rows, features), jnp.bfloat16),
        scratch_shapes=[pltpu.VMEM((rows, features), jnp.float32)],
        compiler_params=pltpu.CompilerParams(vmem_limit_bytes=VMEM_BYTES),
        cost_estimate=pl.CostEstimate(
            flops=2 * slots * lats * degrees * 2 * features,
            bytes_accessed=2 * (lat_basis.size + spectral_state.size + rows * features),
            transcendentals=0,
        ),
        name="to_latitudes",
    )(lat_basis, spectral_state)


def degrees_kernel(basis_ref, rows_ref, out_ref, wide):
    lats = basis_ref.shape[1]
    slot = pl.program_id(0)
    per_lat = rows_ref.shape[0] // lats

    @pl.when(slot == 0)
    def _():
        wide[...] = rows_ref[...].astype(jnp.float32)

    spectrum = jnp.concatenate(
        [wide[pl.ds(2 * slot + k, lats, per_lat), :].astype(jnp.bfloat16) for k in range(2)],
        axis=1,
    )
    out_ref[0] = lax.dot_general(
        basis_ref[0], spectrum, (((0,), (0,)), ((), ())), preferred_element_type=jnp.float32
    )


def to_degrees(lat_basis, rows):
    slots, lats, degrees = lat_basis.shape
    features = rows.shape[1]
    return pl.pallas_call(
        degrees_kernel,
        grid=(slots,),
        in_specs=[
            pl.BlockSpec((1, lats, degrees), lambda s: (s, 0, 0)),
            pl.BlockSpec(memory_space=pltpu.VMEM),
        ],
        out_specs=pl.BlockSpec((1, degrees, 2 * features), lambda s: (s, 0, 0)),
        out_shape=jax.ShapeDtypeStruct((slots, degrees, 2 * features), jnp.float32),
        scratch_shapes=[pltpu.VMEM(rows.shape, jnp.float32)],
        compiler_params=pltpu.CompilerParams(vmem_limit_bytes=VMEM_BYTES),
        cost_estimate=pl.CostEstimate(
            flops=2 * slots * lats * degrees * 2 * features,
            bytes_accessed=2 * (lat_basis.size + rows.size) + 8 * slots * degrees * features,
            transcendentals=0,
        ),
        name="to_degrees",
    )(lat_basis, rows)


def angle_parts(waves, step, count, quarter, longitudes, axis):
    positions = jnp.arange(count, dtype=jnp.int32) * step
    shape = (-1, 1) if axis == 1 else (1, -1)
    phases = waves.reshape(shape) * positions.reshape(shape[::-1])
    phases = (phases + quarter.reshape(shape)) % longitudes
    angles = phases.astype(jnp.float32) * (2.0 * math.pi / longitudes)
    return jnp.cos(angles), jnp.sin(angles)


def table_kernel(hi_cos, hi_sin, lo_cos, lo_sin, hi_cos_t, hi_sin_t, lo_cos_t, lo_sin_t, out, out_t):
    longitudes = out.shape[1]
    width = lo_cos.shape[1]
    for a in range(hi_cos.shape[1]):
        size = min(width, longitudes - a * width)
        block = hi_cos[:, a : a + 1] * lo_cos[...] - hi_sin[:, a : a + 1] * lo_sin[...]
        out[:, a * width : a * width + size] = block[:, :size].astype(out.dtype)
    height = lo_cos_t.shape[0]
    for a in range(hi_cos_t.shape[0]):
        block = hi_cos_t[a : a + 1, :] * lo_cos_t[...] - hi_sin_t[a : a + 1, :] * lo_sin_t[...]
        out_t[a * height : (a + 1) * height, :] = block.astype(out_t.dtype)


def fourier_tables(wave_of_slot, sources, longitudes):
    per_source = wave_of_slot.shape[0] // sources
    waves = (wave_of_slot + 1).reshape(sources, per_source).T.reshape(-1)
    waves = jnp.concatenate([waves, waves])
    terms = waves.shape[0]
    quarter = jnp.arange(terms, dtype=jnp.int32) // (terms // 2) * (longitudes // 4)
    none = jnp.zeros_like(quarter)
    width, height = 128, 32
    kept = -(-(longitudes // 2 + 1) // height) * height
    wide = angle_parts(waves, width, -(-kept // width), quarter, longitudes, 1)
    wide += angle_parts(waves, 1, width, none, longitudes, 1)
    tall = angle_parts(waves, height, kept // height, quarter, longitudes, 0)
    tall += angle_parts(waves, 1, height, none, longitudes, 0)
    return pl.pallas_call(
        table_kernel,
        out_shape=(
            jax.ShapeDtypeStruct((terms, kept), jnp.bfloat16),
            jax.ShapeDtypeStruct((kept, terms), jnp.bfloat16),
        ),
        compiler_params=pltpu.CompilerParams(vmem_limit_bytes=VMEM_BYTES),
        cost_estimate=pl.CostEstimate(
            flops=6 * terms * kept, bytes_accessed=4 * terms * kept, transcendentals=0
        ),
        name="fourier_tables",
    )(*wide, *tall)


def silu(v):
    half = 0.5 * v
    return half + half * jnp.tanh(half)


def columns_kernel(
    sources,
    weight_ref,
    places_ref,
    far_first_ref,
    far_second_ref,
    rows_ref,
    table_ref,
    table_t_ref,
    near_ref,
    first_ref,
    first_bias_ref,
    mid_ref,
    mid_bias_ref,
    last_ref,
    out_ref,
    wide_in,
    wide_out,
    coefficients,
    evens,
    odds,
    far_full,
):
    step = pl.program_id(0)
    features = rows_ref.shape[1]
    terms = table_ref.shape[0] // sources
    kept = table_ref.shape[1]
    stride = rows_ref.shape[0] // sources
    lanes = coefficients.shape[1]
    group = lanes // features
    half = near_ref.shape[0] // group // 2
    split = table_ref.shape[0] // 2

    @pl.when(step == 0)
    def _():
        wide_in[...] = rows_ref[...].astype(jnp.float32)
        far_full[...] = jnp.zeros_like(far_full)
        far_half = far_first_ref.shape[0]
        far = wide_out.at[pl.ds(0, 2 * far_half)]
        far[:far_half, :] = far_first_ref[...].astype(jnp.float32)
        far[far_half:, :] = far_second_ref[...].astype(jnp.float32)
        owners = places_ref.shape[0] // 4
        padded = 2 * far_half // owners
        place_piece(places_ref, 2 * owners, places_ref.shape[1], padded, far, far_full)

    def place_of(q):
        return (q % 2) * split + q // 2 * sources

    for j in range(group):
        lat = step * group + j
        for q in range(terms):
            at = place_of(q)
            coefficients[at : at + sources, j * features : (j + 1) * features] = wide_in[
                pl.ds(terms * lat + q, sources, stride), :
            ].astype(jnp.bfloat16)

    def network(state, start):
        def surface_at(j):
            here = 2 * half * j + start
            at = pl.multiple_of(step * group * 2 * half + here, 16)
            near = near_ref[here : here + half, :].astype(jnp.float32)
            return (near + far_full[pl.ds(at, half), :]).astype(jnp.bfloat16)

        joined = jnp.concatenate(
            [
                jnp.concatenate(
                    [
                        state[:, j * features : (j + 1) * features].astype(jnp.bfloat16),
                        surface_at(j),
                    ],
                    axis=1,
                )
                for j in range(group)
            ],
            axis=0,
        )
        first = jnp.dot(joined, first_ref[...], preferred_element_type=jnp.float32)
        first = silu(first + first_bias_ref[...]).astype(jnp.bfloat16)
        second = jnp.dot(first, mid_ref[...], preferred_element_type=jnp.float32)
        second = silu(second + mid_bias_ref[...]).astype(jnp.bfloat16)
        third = jnp.dot(second, last_ref[...], preferred_element_type=jnp.float32)
        return jnp.concatenate([third[j * half : (j + 1) * half, :] for j in range(group)], axis=1)

    even = jnp.dot(
        table_t_ref[:, :split], coefficients[:split, :], preferred_element_type=jnp.float32
    )
    odd = jnp.dot(
        table_t_ref[:half, split:], coefficients[split:, :], preferred_element_type=jnp.float32
    )
    lone, even = even[half : half + 1, :], even[:half, :]
    top = lax.broadcasted_iota(jnp.int32, (half, lanes), 0) == 0
    east = network(even + odd, 0)
    west = network(jnp.where(top, lone, even - odd), half)
    evens[:half, :] = jnp.where(top, east, east + west).astype(jnp.bfloat16)
    evens[half:, :] = jnp.where(top[: kept - half, :], west[: kept - half, :], 0.0).astype(
        jnp.bfloat16
    )
    odds[:half, :] = (east - west).astype(jnp.bfloat16)
    odds[half:, :] = jnp.zeros((kept - half, lanes), jnp.bfloat16)

    for k, halves in enumerate((evens, odds)):
        spectrum = jnp.dot(
            table_ref[k * split : (k + 1) * split, :],
            halves[...],
            preferred_element_type=jnp.float32,
        )
        for j in range(group):
            lat = step * group + j
            scaled = spectrum[:, j * features : (j + 1) * features] * weight_ref[lat]
            for q in range(k, terms, 2):
                at = q // 2 * sources
                wide_out[pl.ds(terms * lat + q, sources, stride), :] = scaled[at : at + sources, :]

    @pl.when(step == pl.num_programs(0) - 1)
    def _():
        out_ref[...] = wide_out[...].astype(out_ref.dtype)


def column_spectrum(
    rows, tables, surface_rows, quad_weight, sources, first, first_bias, mid, mid_bias, last
):
    table, table_t = tables
    terms, kept = table.shape
    places, near, far_first, far_second = surface_rows
    longitudes = near.shape[0] // quad_weight.shape[0]
    features = rows.shape[1]
    lats = quad_weight.shape[0]
    group = 2 if lats % 2 == 0 else 1
    hidden = first.shape[1]
    columns = lats * longitudes
    flops = 2 * columns * (terms * features + 2 * features * hidden)
    flops += 2 * columns * (hidden * hidden + hidden * features)
    return pl.pallas_call(
        functools.partial(columns_kernel, sources),
        grid=(lats // group,),
        in_specs=[
            pl.BlockSpec(memory_space=pltpu.SMEM),
            pl.BlockSpec(memory_space=pltpu.SMEM),
            whole(far_first.shape),
            whole(far_second.shape),
            whole(rows.shape),
            whole(table.shape),
            whole(table_t.shape),
            pl.BlockSpec((group * longitudes, near.shape[1]), lambda i: (i, 0)),
            whole(first.shape),
            whole((1, hidden)),
            whole(mid.shape),
            whole((1, hidden)),
            whole(last.shape),
        ],
        out_specs=whole(rows.shape),
        out_shape=jax.ShapeDtypeStruct(rows.shape, jnp.bfloat16),
        scratch_shapes=[
            pltpu.VMEM(rows.shape, jnp.float32),
            pltpu.VMEM(rows.shape, jnp.float32),
            pltpu.VMEM((terms, group * features), jnp.bfloat16),
            pltpu.VMEM((kept, group * features), jnp.bfloat16),
            pltpu.VMEM((kept, group * features), jnp.bfloat16),
            pltpu.VMEM((near.shape[0] + 8, near.shape[1]), jnp.float32),
        ],
        compiler_params=pltpu.CompilerParams(vmem_limit_bytes=60 * 1024 * 1024),
        cost_estimate=pl.CostEstimate(
            flops=flops,
            bytes_accessed=2 * (2 * rows.size + 2 * table.size + near.size),
            transcendentals=2 * columns * hidden,
        ),
        name="column_spectrum",
    )(
        quad_weight,
        places,
        far_first,
        far_second,
        rows,
        table,
        table_t,
        near,
        first,
        first_bias.reshape(1, hidden),
        mid,
        mid_bias.reshape(1, hidden),
        last,
    )


def exchange(chunks):
    return lax.all_to_all(chunks, "band", split_axis=0, concat_axis=0, tiled=True)


def fetch_kernel(ids_ref, held_ref, out_ref, wide, found):
    wide[...] = held_ref[...].astype(jnp.float32)
    count = ids_ref.shape[2]

    def one_peer(peer, carry):
        base = pl.multiple_of(peer * count, count)
        for i in range(count):
            found[pl.ds(base + i, 1), :] = wide[pl.ds(ids_ref[peer, 0, i], 1), :]
        return carry

    lax.fori_loop(0, ids_ref.shape[0], one_peer, 0)
    out_ref[...] = found[...].astype(out_ref.dtype)


def fetch_rows(ids, held):
    rows = ids.shape[0] * ids.shape[2]
    features = held.shape[1]
    return pl.pallas_call(
        fetch_kernel,
        in_specs=[pl.BlockSpec(memory_space=pltpu.SMEM), pl.BlockSpec(memory_space=pltpu.VMEM)],
        out_specs=pl.BlockSpec(memory_space=pltpu.VMEM),
        out_shape=jax.ShapeDtypeStruct((rows, features), held.dtype),
        scratch_shapes=[
            pltpu.VMEM(held.shape, jnp.float32),
            pltpu.VMEM((rows, features), jnp.float32),
        ],
        compiler_params=pltpu.CompilerParams(vmem_limit_bytes=VMEM_BYTES),
        cost_estimate=pl.CostEstimate(
            flops=0, bytes_accessed=20 * 2 * (held.size + rows * features), transcendentals=0
        ),
        name="fetch_rows",
    )(ids, held)


def place_piece(places_ref, first, quota, padded, wide, full_ref):
    def one_owner(owner, carry):
        base = pl.multiple_of(owner * padded, padded)
        for i in range(quota):
            full_ref[pl.ds(places_ref[first + owner, i], 1), :] = wide[pl.ds(base + i, 1), :]
        return carry

    lax.fori_loop(0, wide.shape[0] // padded, one_owner, 0)


def near_kernel(padded, places_ref, own_ref, above_ref, below_ref, out_ref, full, wide):
    owners = wide.shape[0] // padded
    full[...] = jnp.zeros_like(full)
    for away, piece in ((0, own_ref), (1, above_ref), (3, below_ref)):
        wide[...] = piece[...].astype(jnp.float32)
        place_piece(places_ref, away * owners, places_ref.shape[1], padded, wide, full)
    out_ref[...] = full[: out_ref.shape[0], :].astype(out_ref.dtype)


def place_near(places, own, above, below, total):
    padded = own.shape[0] // (places.shape[0] // 4)
    features = own.shape[1]
    return pl.pallas_call(
        functools.partial(near_kernel, padded),
        in_specs=[pl.BlockSpec(memory_space=pltpu.SMEM)]
        + [pl.BlockSpec(memory_space=pltpu.VMEM)] * 3,
        out_specs=pl.BlockSpec(memory_space=pltpu.VMEM),
        out_shape=jax.ShapeDtypeStruct((total, features), own.dtype),
        scratch_shapes=[
            pltpu.VMEM((total + 8, features), jnp.float32),
            pltpu.VMEM(own.shape, jnp.float32),
        ],
        compiler_params=pltpu.CompilerParams(vmem_limit_bytes=VMEM_BYTES),
        cost_estimate=pl.CostEstimate(flops=0, bytes_accessed=30 * 2**20, transcendentals=0),
        name="place_near",
    )(places, own, above, below)


def gathered_over_members(places, piece, total, tables):
    members = lax.axis_size("ens")
    up = [(i, (i + 1) % members) for i in range(members)]
    down = [(i, (i - 1) % members) for i in range(members)]
    half = piece.shape[0] // 2
    below = lax.ppermute(piece, "ens", up)
    above = lax.ppermute(piece, "ens", down)
    below, above, tables = lax.optimization_barrier((below, above, tables))
    far_first = lax.ppermute(below[:half], "ens", up)
    far_second = lax.ppermute(above[half:], "ens", down)
    near = place_near(places, piece, above, below, total)
    return (places, near, far_first, far_second), tables


def requests(dest_owner, dest_slot, held):
    owners = lax.axis_size("band")
    members = lax.axis_size("ens")
    total = dest_owner.size
    per_owner = total // owners
    quota = -(-per_owner // members)
    padded = -(-quota // 16) * 16
    columns = jnp.arange(total, dtype=jnp.int32)
    keys = (dest_owner * held + dest_slot).reshape(-1)
    keys, order = lax.sort((keys, columns), num_keys=1)
    slots = keys.reshape(owners, per_owner) - jnp.arange(owners, dtype=jnp.int32)[:, None] * held
    slots = jnp.pad(slots, ((0, 0), (0, quota * members - per_owner)))
    mine = lax.dynamic_slice_in_dim(slots, lax.axis_index("ens") * quota, quota, axis=1)
    mine = jnp.pad(mine, ((0, 0), (0, padded - quota)))
    return mine.reshape(owners, 1, padded), order


def places_of_rows(order, quota, longitudes):
    owners = lax.axis_size("band")
    members = lax.axis_size("ens")
    total = order.shape[0]
    per_owner = total // owners
    across = order % longitudes
    folded = jnp.where(across <= longitudes // 2, across, longitudes * 3 // 2 - across)
    order = order - across + folded
    places = jnp.pad(
        order.reshape(owners, per_owner),
        ((0, 0), (0, quota * members - per_owner)),
        constant_values=total,
    )
    places = places.reshape(owners, members, quota).transpose(1, 0, 2)
    places = jnp.concatenate([places, places], axis=0)
    places = lax.dynamic_slice_in_dim(places, lax.axis_index("ens"), members, axis=0)
    return places.reshape(members * owners, quota)


def local(
    spectral_state,
    lat_basis,
    quad_weight,
    wave_of_slot,
    dest_owner,
    dest_slot,
    surface,
    in_weight,
    surface_weight,
    in_bias,
    mid_weight,
    mid_bias,
    out_weight,
):
    bands = lax.axis_size("band")
    longitudes = dest_owner.shape[1]
    ids, order = requests(dest_owner, dest_slot, surface.shape[0])
    padded = ids.shape[2]
    quota = -(-(order.shape[0] // bands) // lax.axis_size("ens"))
    fourier = to_latitudes(lat_basis, spectral_state)
    replies = fetch_rows(exchange(ids), surface)
    replies, fourier = lax.optimization_barrier((replies, fourier))
    features = fourier.shape[1]
    fetched = exchange(replies.reshape(bands, padded, -1)).reshape(-1, surface.shape[1])
    places = places_of_rows(order, quota, longitudes)
    tables = fourier_tables(wave_of_slot, bands, longitudes)
    surface_rows, tables = gathered_over_members(places, fetched, order.shape[0], tables)
    banded = exchange(fourier.reshape(bands, -1, features)).reshape(-1, features)
    weight = quad_weight * math.sqrt(2.0 / longitudes)
    first = jnp.concatenate([in_weight, surface_weight], axis=0)
    network = (first, in_bias, mid_weight, mid_bias, out_weight)
    spectrum = column_spectrum(banded, tables, surface_rows, weight, bands, *network)
    owned = exchange(spectrum.reshape(bands, -1, features)).reshape(-1, features)
    return to_degrees(lat_basis, owned)


def solution(mesh):
    return jax.shard_map(
        local,
        mesh=mesh,
        in_specs=(
            P(("ens", "band"), None, None),
            P("band", None, None),
            P("band"),
            P(),
            P("band", None),
            P("band", None),
            P("band", None),
            P(),
            P(),
            P(),
            P(),
            P(),
            P(),
        ),
        out_specs=P(("ens", "band"), None, None),
        check_vma=False,
    )
```

profile of v0, /device:TPU:2, one launch (start us, length us, event | category | flops | bytes accessed | tf_op | source)
XLA Modules:
  0.0 215.2 jit_solution(939591850557770326)
XLA Ops:
  0.0 1.0 multiply_add_fusion
  1.0 0.1 reshape.101
  1.1 7.8 %sort.15 = (s32[14400]{0:T(1024)S(1)}, s32[14400]{0:T(1024)}) sort(s32[14400]{0:T(1024)S(1)} %reshape.101, s32[14400]{0:T(1024)S(1)} %iota.35), dimensions={0}, to_apply=%region_0.0 | sort | flops 201600 | bytes 230400 | tf_op jit(solution)/shard_map/sort | solution.py:434
  8.9 0.2 reshape.105
  9.1 0.1 broadcast_subtract_fusion
  9.2 0.1 pad_dynamic-slice_fusion.2
  9.2 0.6 pad.13
  9.9 12.0 %all-to-all-start = ((s32[64,1,64]{2,1,0:T(1,128)}), s32[64,1,64]{2,1,0:T(1,128)S(1)}, u32[]{:S(2)}, u32[]{:S(2)}) async-start(s32[64,1,64]{2,1,0:T(1,128)} %bitcast.2), calls=%async_computation | async-start | bytes 65536 | tf_op jit(solution)/shard_map/all_to_all | solution.py:336
  21.9 0.0 copy-start
  21.9 1.8 copy-done
  23.7 0.0 copy-start.4
  23.7 1.3 copy-done.4
  25.0 3.5 %to_latitudes.1 = bf16[7680,128]{1,0:T(8,128)(2,1)} custom-call(bf16[6,640,384]{2,1,0:T(8,128)(2,1)S(1)} %copy-done, bf16[6,384,256]{2,1,0:T(8,128)(2,1)S(1)} %copy-done.4), custom_call_target="tpu_custom_call" | custom-call | flops 754974720 | bytes 6094848 | tf_op jit(solution)/shard_map/to_latitudes/pallas_call | solution.py:36
  28.5 2.0 all-to-all-done.ids_ref
  30.5 0.0 copy-start.2
  30.5 2.0 copy-done.2
  32.5 5.2 %fetch_rows.1 = bf16[4096,128]{1,0:T(8,128)(2,1)S(1)} custom-call(s32[64,1,64]{2,1,0:T(1,128)S(1)} %all-to-all-done.ids_ref, bf16[14400,128]{1,0:T(8,128)(2,1)S(1)} %copy-done.2), custom_call_target="tpu_custom_call" | custom-call | bytes 94699520 | tf_op jit(solution)/shard_map/fetch_rows/pallas_call | solution.py:356
  37.7 36.9 %all_to_all.20 = bf16[64,64,128]{2,1,0:T(8,128)(2,1)S(1)} all-to-all(bf16[64,64,128]{2,1,0:T(8,128)(2,1)S(1)} %bitcast.16), channel_id=1, replica_groups=mesh['ens'=4,'band'=64] {'band'}, dimensions={0} | all-to-all | bytes 2097152 | tf_op jit(solution)/shard_map/all_to_all | solution.py:336
  74.6 6.0 %all-to-all-start.2 = ((bf16[64,120,128]{2,1,0:T(8,128)(2,1)}), bf16[64,120,128]{2,1,0:T(8,128)(2,1)}, u32[]{:S(2)}, u32[]{:S(2)}) async-start(bf16[64,120,128]{2,1,0:T(8,128)(2,1)} %bitcast.6), calls=%async_computation.2 | async-start | bytes 3932160 | tf_op jit(solution)/shard_map/all_to_all | solution.py:336
  80.6 0.0 copy-done.11
  80.6 0.1 reshape.109
  80.7 0.1 copy.17
  80.8 0.1 reshape.110
  80.9 0.1 fusion.23
  81.0 0.2 copy.18
  81.2 1.7 collective-permute-start
  82.9 1.7 collective-permute-start.1
  84.6 0.4 fusion.19
  85.0 0.4 fusion.12
  85.4 1.7 fusion.4
  87.1 1.4 multiply_sine_fusion
  88.5 0.0 copy-start.10
  88.5 1.6 fourier_tables.1
  90.1 0.0 copy-start.6
  90.1 1.0 copy-done.6
  91.2 1.0 copy-done.7
  92.2 15.6 %collective-permute-done.below_ref = bf16[4096,128]{1,0:T(8,128)(2,1)S(1)} collective-permute-done((bf16[4096,128]{1,0:T(8,128)(2,1)S(1)}, bf16[4096,128]{1,0:T(8,128)(2,1)S(1)}, u32[]{:S(2)}, u32[]{:S(2)}) %collective-permute-start) | collective-permute-done | bytes 1048608 | tf_op jit(solution)/shard_map/ppermute | solution.py:416
  107.8 0.0 collective-permute-done.1.above_ref
  107.8 0.8 slice.6
  108.6 1.6 collective-permute-start.2
  110.2 0.8 slice.7
  111.0 1.7 collective-permute-start.3
  112.7 0.0 copy-done.10
  112.7 0.1 fusion.22
  112.8 0.2 reshape.102
  113.0 0.1 reshape.103
  113.1 0.1 fusion.7
  113.3 0.0 copy-done.8
  113.3 0.0 copy-done.9
  113.3 0.0 copy-start.5
  113.3 0.7 pad_maximum_fusion.first_ref
  114.0 0.0 copy-done.12
  114.0 0.5 broadcast_multiply_fusion.weight_ref
  114.5 13.5 %place_near.1.near_ref = bf16[14400,128]{1,0:T(8,128)(2,1)S(1)} custom-call(s32[256,57]{1,0:T(8,128)S(1)} %bitcast.17, bf16[4096,128]{1,0:T(8,128)(2,1)S(1)} %bitcast.15, bf16[4096,128]{1,0:T(8,128)(2,1)S(1)} %collective-permute-done.1.above_ref, bf16[4096,128]{1,0:T(8,128)(2,1)S(1)} %collective-permute-done.below_ref), custom_call_target="tpu_custom_call" | custom-call | bytes 31457280 | tf_op jit(solution)/shard_map/place_near/pallas_call | solution.py:395
  128.0 0.0 copy-done.5
  128.0 0.0 copy-start.3
  128.0 1.8 copy-done.3
  129.8 0.0 collective-permute-done.2.far_first_ref
  129.8 0.0 collective-permute-done.3.far_second_ref
  129.8 0.0 all-to-all-done.2
  129.8 22.4 %column_spectrum.1 = bf16[7680,128]{1,0:T(8,128)(2,1)} custom-call(f32[10]{0:T(128)} %broadcast_multiply_fusion.weight_ref, s32[256,57]{1,0:T(8,128)} %bitcast.18, bf16[2048,128]{1,0:T(8,128)(2,1)} %collective-permute-done.2.far_first_ref, bf16[2048,128]{1,0:T(8,128)(2,1)} %collective-permute-done.3.far_second_ref, bf16[7680,128]{1,0:T(8,128)(2,1)} %bitcast.7.rows_ref, ...), custom_call_target="tpu_custom_call" | custom-call | flops 7549747200 | bytes 9879552 | tf_op jit(solution)/shard_map/column_spectrum/pallas_call | solution.py:283
  152.3 59.0 %all_to_all.21 = bf16[64,120,128]{2,1,0:T(8,128)(2,1)S(1)} all-to-all(bf16[64,120,128]{2,1,0:T(8,128)(2,1)} %bitcast.19), channel_id=1, replica_groups=mesh['ens'=4,'band'=64] {'band'}, dimensions={0} | all-to-all | bytes 3932160 | tf_op jit(solution)/shard_map/all_to_all | solution.py:336
  211.3 0.0 copy-done.1
  211.3 4.0 %to_degrees.1 = f32[6,384,256]{2,1,0:T(8,128)} custom-call(bf16[6,640,384]{2,1,0:T(8,128)(2,1)S(1)} %copy-done.1, bf16[7680,128]{1,0:T(8,128)(2,1)S(1)} %bitcast.12), custom_call_target="tpu_custom_call" | custom-call | flops 754974720 | bytes 7274496 | tf_op jit(solution)/shard_map/to_degrees/pallas_call | solution.py:77
  (17 shorter events, 0.1 us)
Async XLA Ops:
  9.9 20.6 %all-to-all-start = ((s32[64,1,64]{2,1,0:T(1,128)}), s32[64,1,64]{2,1,0:T(1,128)S(1)}, u32[]{:S(2)}, u32[]{:S(2)}) async-start(s32[64,1,64]{2,1,0:T(1,128)} %bitcast.2), calls=%async_computation | async-start | bytes 65536 | tf_op jit(solution)/shard_map/all_to_all | solution.py:336
  21.9 1.8 copy-start
  23.7 1.3 copy-start.4
  30.5 2.0 copy-start.2
  74.6 6.0 %copy-start.11 = (s32[384]{0:T(512)S(1)}, s32[384]{0:T(512)}, u32[]{:S(2)}) copy-start(s32[384]{0:T(512)} %param.16) | copy-start | bytes 4612
  74.6 55.2 %all-to-all-start.2 = ((bf16[64,120,128]{2,1,0:T(8,128)(2,1)}), bf16[64,120,128]{2,1,0:T(8,128)(2,1)}, u32[]{:S(2)}, u32[]{:S(2)}) async-start(bf16[64,120,128]{2,1,0:T(8,128)(2,1)} %bitcast.6), calls=%async_computation.2 | async-start | bytes 3932160 | tf_op jit(solution)/shard_map/all_to_all | solution.py:336
  81.2 26.6 %collective-permute-start = (bf16[4096,128]{1,0:T(8,128)(2,1)S(1)}, bf16[4096,128]{1,0:T(8,128)(2,1)S(1)}, u32[]{:S(2)}, u32[]{:S(2)}) collective-permute-start(bf16[4096,128]{1,0:T(8,128)(2,1)S(1)} %bitcast.13), channel_id=1, source_target_pairs={{0,64},{64,128},{128,192},{192,0},{1,65},{65,129},{129,193},{193,1... | collective-permute-start | bytes 3145736 | tf_op jit(solution)/shard_map/ppermute | solution.py:416
  82.9 24.9 %collective-permute-start.1 = (bf16[4096,128]{1,0:T(8,128)(2,1)S(1)}, bf16[4096,128]{1,0:T(8,128)(2,1)S(1)}, u32[]{:S(2)}, u32[]{:S(2)}) collective-permute-start(bf16[4096,128]{1,0:T(8,128)(2,1)S(1)} %bitcast.14), channel_id=1, source_target_pairs={{0,192},{64,0},{128,64},{192,128},{1,193},{65,1},{129,65},{193,129... | collective-permute-start | bytes 3145736 | tf_op jit(solution)/shard_map/ppermute | solution.py:417
  88.5 24.2 %copy-start.10 = (s32[14400]{0:T(1024)S(1)}, s32[14400]{0:T(1024)}, u32[]{:S(2)}) copy-start(s32[14400]{0:T(1024)} %get-tuple-element.15) | copy-start | bytes 172804
  90.1 1.0 copy-start.6
  91.2 1.0 copy-start.7
  92.2 21.1 %copy-start.8 = (bf16[128,256]{1,0:T(8,128)(2,1)S(1)}, bf16[128,256]{1,0:T(8,128)(2,1)}, u32[]{:S(2)}) copy-start(bf16[128,256]{1,0:T(8,128)(2,1)} %param.21) | copy-start | bytes 196612
  92.2 21.1 %copy-start.9 = (bf16[128,256]{1,0:T(8,128)(2,1)S(1)}, bf16[128,256]{1,0:T(8,128)(2,1)}, u32[]{:S(2)}) copy-start(bf16[128,256]{1,0:T(8,128)(2,1)} %param.20) | copy-start | bytes 196612
  92.2 21.8 %copy-start.12 = (f32[10]{0:T(128)S(1)}, f32[10]{0:T(128)}, u32[]{:S(2)}) copy-start(f32[10]{0:T(128)} %param.15) | copy-start | bytes 124
  108.6 21.2 %collective-permute-start.2 = (bf16[2048,128]{1,0:T(8,128)(2,1)}, bf16[2048,128]{1,0:T(8,128)(2,1)}, u32[]{:S(2)}, u32[]{:S(2)}) collective-permute-start(bf16[2048,128]{1,0:T(8,128)(2,1)} %slice.6), channel_id=1, source_target_pairs={{0,64},{64,128},{128,192},{192,0},{1,65},{65,129},{129,193},{193,1... | collective-permute-start | bytes 1572872 | tf_op jit(solution)/shard_map/ppermute | solution.py:419
  111.0 18.8 %collective-permute-start.3 = (bf16[2048,128]{1,0:T(8,128)(2,1)}, bf16[2048,128]{1,0:T(8,128)(2,1)}, u32[]{:S(2)}, u32[]{:S(2)}) collective-permute-start(bf16[2048,128]{1,0:T(8,128)(2,1)} %slice.7), channel_id=1, source_target_pairs={{0,192},{64,0},{128,64},{192,128},{1,193},{65,1},{129,65},{193,129... | collective-permute-start | bytes 1572872 | tf_op jit(solution)/shard_map/ppermute | solution.py:420
  113.3 14.7 %copy-start.5 = (s32[4,64,57]{2,1,0:T(8,128)}, s32[4,64,57]{2,1,0:T(8,128)S(1)}, u32[]{:S(2)}) copy-start(s32[4,64,57]{2,1,0:T(8,128)S(1)} %copy.16) | copy-start | bytes 175108
  128.0 1.8 copy-start.3
  152.3 59.0 %copy-start.1 = (bf16[6,640,384]{2,1,0:T(8,128)(2,1)S(1)}, bf16[6,640,384]{2,1,0:T(8,128)(2,1)}, u32[]{:S(2)}) copy-start(bf16[6,640,384]{2,1,0:T(8,128)(2,1)} %basis_ref.3) | copy-start | bytes 8847364
where the time goes:
time: 216 us; the launch traced here: 215 us
  blocking collectives  95.9 us (44%)
  Pallas kernels  50.1 us (23%)
  starting transfers between devices  24.6 us (11%)
  waiting for transfers between devices  17.6 us (8%)
  other arithmetic  14.3 us (7%)
  local copies, waits for them, and re-layouts  12.4 us (6%)
    all_to_all x2, blocking collectives, exchange(): lax.all_to_all(chunks, 'band', split_axis=0, concat_axis=0, tiled=True)  95.9 us
    pallas_call x1, Pallas kernels, column_spectrum(): pl.pallas_call(functools.partial(columns_kernel, sources), grid=(lats //...  22.4 us
    all_to_all x2, starting transfers between devices, exchange(): lax.all_to_all(chunks, 'band', split_axis=0, concat_axis=0, tiled=True)  18 us
    ppermute x1, waiting for transfers between devices, gathered_over_members(): below = lax.ppermute(piece, 'ens', up)  15.6 us
    pallas_call x1, Pallas kernels, place_near(): pl.pallas_call(functools.partial(near_kernel, padded), in_specs=[pl.Block...  13.5 us
    unnamed x27, local copies, waits for them, and re-layouts  8.96 us
    sort x1, other arithmetic, requests(): keys, order = lax.sort((keys, columns), num_keys=1)  7.82 us
    pallas_call x1, Pallas kernels, fetch_rows(): pl.pallas_call(fetch_kernel, in_specs=[pl.BlockSpec(memory_space=pltpu.SM...  5.18 us
  transfers between devices with their start and end apart: 6, of which 2 were waited for; matrix products, arithmetic and copies ran while one was open for 4% of the time, Pallas kernels for 9%

commit v1 on v0

--- a/solution.py
+++ b/solution.py
@@ -55,33 +55,37 @@
 
 def degrees_kernel(basis_ref, rows_ref, out_ref, wide):
     lats = basis_ref.shape[1]
-    slot = pl.program_id(0)
+    together = basis_ref.shape[0]
+    step = pl.program_id(0)
     per_lat = rows_ref.shape[0] // lats
 
-    @pl.when(slot == 0)
+    @pl.when(step == 0)
     def _():
         wide[...] = rows_ref[...].astype(jnp.float32)
 
-    spectrum = jnp.concatenate(
-        [wide[pl.ds(2 * slot + k, lats, per_lat), :].astype(jnp.bfloat16) for k in range(2)],
-        axis=1,
-    )
-    out_ref[0] = lax.dot_general(
-        basis_ref[0], spectrum, (((0,), (0,)), ((), ())), preferred_element_type=jnp.float32
-    )
+    for i in range(together):
+        slot = step * together + i
+        spectrum = jnp.concatenate(
+            [wide[pl.ds(2 * slot + k, lats, per_lat), :].astype(jnp.bfloat16) for k in range(2)],
+            axis=1,
+        )
+        out_ref[i] = lax.dot_general(
+            basis_ref[i], spectrum, (((0,), (0,)), ((), ())), preferred_element_type=jnp.float32
+        )
 
 
 def to_degrees(lat_basis, rows):
     slots, lats, degrees = lat_basis.shape
     features = rows.shape[1]
+    together = 2 if slots % 2 == 0 else 1
     return pl.pallas_call(
         degrees_kernel,
-        grid=(slots,),
+        grid=(slots // together,),
         in_specs=[
-            pl.BlockSpec((1, lats, degrees), lambda s: (s, 0, 0)),
+            pl.BlockSpec((together, lats, degrees), lambda s: (s, 0, 0)),
             pl.BlockSpec(memory_space=pltpu.VMEM),
         ],
-        out_specs=pl.BlockSpec((1, degrees, 2 * features), lambda s: (s, 0, 0)),
+        out_specs=pl.BlockSpec((together, degrees, 2 * features), lambda s: (s, 0, 0)),
         out_shape=jax.ShapeDtypeStruct((slots, degrees, 2 * features), jnp.float32),
         scratch_shapes=[pltpu.VMEM(rows.shape, jnp.float32)],
         compiler_params=pltpu.CompilerParams(vmem_limit_bytes=VMEM_BYTES),
@@ -380,22 +384,27 @@
     lax.fori_loop(0, wide.shape[0] // padded, one_owner, 0)
 
 
-def near_kernel(padded, places_ref, own_ref, above_ref, below_ref, out_ref, full, wide):
+def near_kernel(
+    padded, places_ref, own_ref, above_a, above_b, below_a, below_b, out_ref, full, wide
+):
     owners = wide.shape[0] // padded
     full[...] = jnp.zeros_like(full)
-    for away, piece in ((0, own_ref), (1, above_ref), (3, below_ref)):
-        wide[...] = piece[...].astype(jnp.float32)
+    for away, pieces in ((0, (own_ref,)), (1, (above_a, above_b)), (3, (below_a, below_b))):
+        at = 0
+        for piece in pieces:
+            wide[at : at + piece.shape[0], :] = piece[...].astype(jnp.float32)
+            at += piece.shape[0]
         place_piece(places_ref, away * owners, places_ref.shape[1], padded, wide, full)
     out_ref[...] = full[: out_ref.shape[0], :].astype(out_ref.dtype)
 
 
-def place_near(places, own, above, below, total):
+def place_near(places, own, others, total):
     padded = own.shape[0] // (places.shape[0] // 4)
     features = own.shape[1]
     return pl.pallas_call(
         functools.partial(near_kernel, padded),
         in_specs=[pl.BlockSpec(memory_space=pltpu.SMEM)]
-        + [pl.BlockSpec(memory_space=pltpu.VMEM)] * 3,
+        + [pl.BlockSpec(memory_space=pltpu.VMEM)] * 5,
         out_specs=pl.BlockSpec(memory_space=pltpu.VMEM),
         out_shape=jax.ShapeDtypeStruct((total, features), own.dtype),
         scratch_shapes=[
@@ -405,7 +414,7 @@
         compiler_params=pltpu.CompilerParams(vmem_limit_bytes=VMEM_BYTES),
         cost_estimate=pl.CostEstimate(flops=0, bytes_accessed=30 * 2**20, transcendentals=0),
         name="place_near",
-    )(places, own, above, below)
+    )(places, own, *others)
 
 
 def gathered_over_members(places, piece, total, tables):
@@ -413,13 +422,16 @@
     up = [(i, (i + 1) % members) for i in range(members)]
     down = [(i, (i - 1) % members) for i in range(members)]
     half = piece.shape[0] // 2
-    below = lax.ppermute(piece, "ens", up)
-    above = lax.ppermute(piece, "ens", down)
-    below, above, tables = lax.optimization_barrier((below, above, tables))
-    far_first = lax.ppermute(below[:half], "ens", up)
-    far_second = lax.ppermute(above[half:], "ens", down)
-    near = place_near(places, piece, above, below, total)
-    return (places, near, far_first, far_second), tables
+    first, second = piece[:half], piece[half:]
+    below_a = lax.ppermute(first, "ens", up)
+    above_b = lax.ppermute(second, "ens", down)
+    below_b = lax.ppermute(second, "ens", up)
+    above_a = lax.ppermute(first, "ens", down)
+    far_a = lax.ppermute(below_a, "ens", up)
+    far_b = lax.ppermute(above_b, "ens", down)
+    below_b, above_a, tables = lax.optimization_barrier((below_b, above_a, tables))
+    near = place_near(places, piece, (above_a, above_b, below_a, below_b), total)
+    return (places, near, far_a, far_b), tables
 
 
 def requests(dest_owner, dest_slot, held):

time: 216 us -> 211 us (0.977)
  waiting for transfers between devices: 17.6 us -> 14.4 us
  starting transfers between devices: 24.6 us -> 27.8 us
    ppermute x4 -> x6, waiting for transfers between devices: 15.6 us -> 10.4 us  [the longest x1 6.03 us: gathered_over_members(): below_a = lax.ppermute(first, 'ens', up)]
    ppermute x4 -> x6, starting transfers between devices: 6.6 us -> 9.79 us  [the longest x1 2.87 us: gathered_over_members(): above_a = lax.ppermute(first, 'ens', down)]
  transfers between devices with their start and end apart: 6 -> 8, of which waited for: 2 -> 6; matrix products, arithmetic and copies ran while one was open for 4% -> 3% of each run, Pallas kernels for 9% -> 9%
where the time goes in v1:
time: 211 us
  blocking collectives  93.9 us (45%)
  Pallas kernels  49.2 us (23%)
  starting transfers between devices  27.8 us (13%)
  waiting for transfers between devices  14.4 us (7%)
  other arithmetic  13.7 us (6%)
  local copies, waits for them, and re-layouts  11.5 us (5%)
    all_to_all x2, blocking collectives, exchange(): lax.all_to_all(chunks, 'band', split_axis=0, concat_axis=0, tiled=True)  93.9 us
    pallas_call x1, Pallas kernels, column_spectrum(): pl.pallas_call(functools.partial(columns_kernel, sources), grid=(lats //...  22.4 us
    all_to_all x2, starting transfers between devices, exchange(): lax.all_to_all(chunks, 'band', split_axis=0, concat_axis=0, tiled=True)  18 us
    pallas_call x1, Pallas kernels, place_near(): pl.pallas_call(functools.partial(near_kernel, padded), in_specs=[pl.Block...  13.5 us
    unnamed x27, local copies, waits for them, and re-layouts  8.84 us
    sort x1, other arithmetic, requests(): keys, order = lax.sort((keys, columns), num_keys=1)  7.19 us
    ppermute x1, waiting for transfers between devices, gathered_over_members(): below_a = lax.ppermute(first, 'ens', up)  6.03 us
    pallas_call x1, Pallas kernels, fetch_rows(): pl.pallas_call(fetch_kernel, in_specs=[pl.BlockSpec(memory_space=pltpu.SM...  5.18 us
  transfers between devices with their start and end apart: 8, of which 6 were waited for; matrix products, arithmetic and copies ran while one was open for 3% of the time, Pallas kernels for 9%

profile of v1, /device:TPU:2, one launch (start us, length us, event | category | flops | bytes accessed | tf_op | source)
XLA Modules:
  0.0 210.8 jit_solution(11263244858817617866)
XLA Ops:
  0.0 1.0 multiply_add_fusion
  1.0 0.1 reshape.103
  1.1 7.2 %sort.15 = (s32[14400]{0:T(1024)S(1)}, s32[14400]{0:T(1024)S(1)}) sort(s32[14400]{0:T(1024)S(1)} %reshape.103, s32[14400]{0:T(1024)S(1)} %iota.35), dimensions={0}, to_apply=%region_0.0 | sort | flops 201600 | bytes 230400 | tf_op jit(solution)/shard_map/sort | solution.py:446
  8.3 0.2 reshape.107
  8.5 0.1 broadcast_subtract_fusion
  8.5 0.1 pad_dynamic-slice_fusion.2
  8.6 0.6 pad.13
  9.2 12.0 %all-to-all-start = ((s32[64,1,64]{2,1,0:T(1,128)}), s32[64,1,64]{2,1,0:T(1,128)S(1)}, u32[]{:S(2)}, u32[]{:S(2)}) async-start(s32[64,1,64]{2,1,0:T(1,128)} %bitcast.2), calls=%async_computation | async-start | bytes 65536 | tf_op jit(solution)/shard_map/all_to_all | solution.py:340
  21.3 0.0 copy-start
  21.3 1.8 copy-done
  23.1 1.3 copy-done.4
  24.4 3.5 %to_latitudes.1 = bf16[7680,128]{1,0:T(8,128)(2,1)} custom-call(bf16[6,640,384]{2,1,0:T(8,128)(2,1)S(1)} %copy-done, bf16[6,384,256]{2,1,0:T(8,128)(2,1)S(1)} %copy-done.4), custom_call_target="tpu_custom_call" | custom-call | flops 754974720 | bytes 6094848 | tf_op jit(solution)/shard_map/to_latitudes/pallas_call | solution.py:36
  27.8 2.0 all-to-all-done.ids_ref
  29.8 2.0 copy-done.2
  31.9 5.2 %fetch_rows.1 = bf16[4096,128]{1,0:T(8,128)(2,1)S(1)} custom-call(s32[64,1,64]{2,1,0:T(1,128)S(1)} %all-to-all-done.ids_ref, bf16[14400,128]{1,0:T(8,128)(2,1)S(1)} %copy-done.2), custom_call_target="tpu_custom_call" | custom-call | bytes 94699520 | tf_op jit(solution)/shard_map/fetch_rows/pallas_call | solution.py:360
  37.1 36.9 %all_to_all.20 = bf16[64,64,128]{2,1,0:T(8,128)(2,1)S(1)} all-to-all(bf16[64,64,128]{2,1,0:T(8,128)(2,1)S(1)} %bitcast.16), channel_id=1, replica_groups=mesh['ens'=4,'band'=64] {'band'}, dimensions={0} | all-to-all | bytes 2097152 | tf_op jit(solution)/shard_map/all_to_all | solution.py:340
  74.0 6.0 %all-to-all-start.2 = ((bf16[64,120,128]{2,1,0:T(8,128)(2,1)}), bf16[64,120,128]{2,1,0:T(8,128)(2,1)}, u32[]{:S(2)}, u32[]{:S(2)}) async-start(bf16[64,120,128]{2,1,0:T(8,128)(2,1)} %bitcast.6), calls=%async_computation.2 | async-start | bytes 3932160 | tf_op jit(solution)/shard_map/all_to_all | solution.py:340
  79.9 0.0 copy-done.10
  80.0 0.1 reshape.112
  80.1 0.1 copy.17
  80.2 0.1 reshape.113
  80.3 0.1 fusion.22
  80.3 0.2 reshape.104
  80.5 0.1 reshape.105
  80.7 0.1 fusion.7
  80.9 0.1 fusion.23
  81.0 0.4 fusion.12
  81.4 0.9 fusion.31
  82.3 1.6 collective-permute-start
  83.8 1.7 collective-permute-start.2
  85.5 0.2 copy.18
  85.7 0.0 copy-start.5
  85.7 0.0 copy-start.8
  85.7 0.0 copy-start.9
  85.7 0.0 copy-start.12
  85.8 1.7 fusion.4
  87.4 1.4 multiply_sine_fusion
  88.9 0.4 collective-permute-start.4
  89.3 2.9 %collective-permute-start.5 = (bf16[2048,128]{1,0:T(8,128)(2,1)S(1)}, bf16[2048,128]{1,0:T(8,128)(2,1)S(1)}, u32[]{:S(2)}, u32[]{:S(2)}) collective-permute-start(bf16[2048,128]{1,0:T(8,128)(2,1)S(1)} %bitcast.22), channel_id=1, source_target_pairs={{0,192},{64,0},{128,64},{192,128},{1,193},{65,1},{129,65},{193,129... | collective-permute-start | bytes 1572872 | tf_op jit(solution)/shard_map/ppermute | solution.py:429
  92.2 6.0 %collective-permute-done.below_a = bf16[2048,128]{1,0:T(8,128)(2,1)S(1)} collective-permute-done((bf16[2048,128]{1,0:T(8,128)(2,1)S(1)}, bf16[2048,128]{1,0:T(8,128)(2,1)S(1)}, u32[]{:S(2)}, u32[]{:S(2)}) %collective-permute-start) | collective-permute-done | bytes 524320 | tf_op jit(solution)/shard_map/ppermute | solution.py:426
  98.2 0.4 collective-permute-start.1
  98.6 0.2 collective-permute-done.2.above_b
  98.9 2.9 %collective-permute-start.3 = (bf16[2048,128]{1,0:T(8,128)(2,1)S(1)}, bf16[2048,128]{1,0:T(8,128)(2,1)}, u32[]{:S(2)}, u32[]{:S(2)}) collective-permute-start(bf16[2048,128]{1,0:T(8,128)(2,1)S(1)} %collective-permute-done.2.above_b), channel_id=1, source_target_pairs={{0,192},{64,0},{128,64},{192,128},{1,193},{65,1},{129,65},{193,129... | collective-permute-start | bytes 1572872 | tf_op jit(solution)/shard_map/ppermute | solution.py:431
  101.7 0.4 fusion.19
  102.1 1.6 fourier_tables.1
  103.7 0.0 copy-start.7
  103.7 1.0 copy-done.7
  104.7 0.0 copy-done.8
  104.7 0.0 copy-done.9
  104.7 0.7 pad_maximum_fusion.first_ref
  105.4 0.0 copy-done.12
  105.4 0.6 broadcast_multiply_fusion.weight_ref
  106.0 3.5 %collective-permute-done.4.below_b = bf16[2048,128]{1,0:T(8,128)(2,1)S(1)} collective-permute-done((bf16[2048,128]{1,0:T(8,128)(2,1)}, bf16[2048,128]{1,0:T(8,128)(2,1)S(1)}, u32[]{:S(2)}, u32[]{:S(2)}) %collective-permute-start.4) | collective-permute-done | bytes 524320 | tf_op jit(solution)/shard_map/ppermute | solution.py:428
  109.5 0.6 collective-permute-done.5.above_a
  110.1 0.0 copy-done.5
  110.1 13.5 %place_near.1.near_ref = bf16[14400,128]{1,0:T(8,128)(2,1)S(1)} custom-call(s32[256,57]{1,0:T(8,128)S(1)} %bitcast.17, bf16[4096,128]{1,0:T(8,128)(2,1)S(1)} %bitcast.14, bf16[2048,128]{1,0:T(8,128)(2,1)S(1)} %collective-permute-done.5.above_a, bf16[2048,128]{1,0:T(8,128)(2,1)S(1)} %collective-permute-done.2.above_b, ...), custom_call_target="tpu_custom_call" | custom-call | bytes 31457280 | tf_op jit(solution)/shard_map/place_near/pallas_call | solution.py:404
  123.6 1.8 copy-done.3
  125.4 0.0 collective-permute-done.1.far_first_ref
  125.4 0.9 copy-done.11
  126.3 0.0 collective-permute-done.3.far_second_ref
  126.3 2.1 all-to-all-done.2
  128.3 22.4 %column_spectrum.1 = bf16[7680,128]{1,0:T(8,128)(2,1)} custom-call(f32[10]{0:T(128)} %broadcast_multiply_fusion.weight_ref, s32[256,57]{1,0:T(8,128)} %bitcast.18, bf16[2048,128]{1,0:T(8,128)(2,1)} %copy-done.11, bf16[2048,128]{1,0:T(8,128)(2,1)} %collective-permute-done.3.far_second_ref, bf16[7680,128]{1,0:T(8,128)(2,1)} %bitcast.7.rows_ref, ...), custom_call_target="tpu_custom_call" | custom-call | flops 7549747200 | bytes 9879552 | tf_op jit(solution)/shard_map/column_spectrum/pallas_call | solution.py:287
  150.7 57.0 %all_to_all.21 = bf16[64,120,128]{2,1,0:T(8,128)(2,1)S(1)} all-to-all(bf16[64,120,128]{2,1,0:T(8,128)(2,1)} %bitcast.19), channel_id=1, replica_groups=mesh['ens'=4,'band'=64] {'band'}, dimensions={0} | all-to-all | bytes 3932160 | tf_op jit(solution)/shard_map/all_to_all | solution.py:340
  207.7 3.0 %to_degrees.1 = f32[6,384,256]{2,1,0:T(8,128)} custom-call(bf16[6,640,384]{2,1,0:T(8,128)(2,1)S(1)} %copy-done.1, bf16[7680,128]{1,0:T(8,128)(2,1)S(1)} %bitcast.15), custom_call_target="tpu_custom_call" | custom-call | flops 754974720 | bytes 7274496 | tf_op jit(solution)/shard_map/to_degrees/pallas_call | solution.py:81
  (20 shorter events, 0.1 us)
Async XLA Ops:
  9.2 20.6 %all-to-all-start = ((s32[64,1,64]{2,1,0:T(1,128)}), s32[64,1,64]{2,1,0:T(1,128)S(1)}, u32[]{:S(2)}, u32[]{:S(2)}) async-start(s32[64,1,64]{2,1,0:T(1,128)} %bitcast.2), calls=%async_computation | async-start | bytes 65536 | tf_op jit(solution)/shard_map/all_to_all | solution.py:340
  21.3 1.8 copy-start
  23.1 1.3 copy-start.4
  29.8 2.0 copy-start.2
  74.0 6.0 %copy-start.10 = (s32[384]{0:T(512)S(1)}, s32[384]{0:T(512)}, u32[]{:S(2)}) copy-start(s32[384]{0:T(512)} %param.16) | copy-start | bytes 4612
  74.0 54.4 %all-to-all-start.2 = ((bf16[64,120,128]{2,1,0:T(8,128)(2,1)}), bf16[64,120,128]{2,1,0:T(8,128)(2,1)}, u32[]{:S(2)}, u32[]{:S(2)}) async-start(bf16[64,120,128]{2,1,0:T(8,128)(2,1)} %bitcast.6), calls=%async_computation.2 | async-start | bytes 3932160 | tf_op jit(solution)/shard_map/all_to_all | solution.py:340
  82.3 16.0 %collective-permute-start = (bf16[2048,128]{1,0:T(8,128)(2,1)S(1)}, bf16[2048,128]{1,0:T(8,128)(2,1)S(1)}, u32[]{:S(2)}, u32[]{:S(2)}) collective-permute-start(bf16[2048,128]{1,0:T(8,128)(2,1)S(1)} %bitcast.21), channel_id=1, source_target_pairs={{0,64},{64,128},{128,192},{192,0},{1,65},{65,129},{129,193},{193,1... | collective-permute-start | bytes 1572872 | tf_op jit(solution)/shard_map/ppermute | solution.py:426
  83.8 15.0 %collective-permute-start.2 = (bf16[2048,128]{1,0:T(8,128)(2,1)}, bf16[2048,128]{1,0:T(8,128)(2,1)S(1)}, u32[]{:S(2)}, u32[]{:S(2)}) collective-permute-start(bf16[2048,128]{1,0:T(8,128)(2,1)} %bitcast.5), channel_id=1, source_target_pairs={{0,192},{64,0},{128,64},{192,128},{1,193},{65,1},{129,65},{193,129... | collective-permute-start | bytes 1572872 | tf_op jit(solution)/shard_map/ppermute | solution.py:427
  85.7 24.4 %copy-start.5 = (s32[4,64,57]{2,1,0:T(8,128)}, s32[4,64,57]{2,1,0:T(8,128)S(1)}, u32[]{:S(2)}) copy-start(s32[4,64,57]{2,1,0:T(8,128)S(1)} %copy.16) | copy-start | bytes 175108
  85.7 19.0 %copy-start.8 = (bf16[128,256]{1,0:T(8,128)(2,1)S(1)}, bf16[128,256]{1,0:T(8,128)(2,1)}, u32[]{:S(2)}) copy-start(bf16[128,256]{1,0:T(8,128)(2,1)} %param.21) | copy-start | bytes 196612
  85.7 19.0 %copy-start.9 = (bf16[128,256]{1,0:T(8,128)(2,1)S(1)}, bf16[128,256]{1,0:T(8,128)(2,1)}, u32[]{:S(2)}) copy-start(bf16[128,256]{1,0:T(8,128)(2,1)} %param.20) | copy-start | bytes 196612
  85.7 19.7 %copy-start.12 = (f32[10]{0:T(128)S(1)}, f32[10]{0:T(128)}, u32[]{:S(2)}) copy-start(f32[10]{0:T(128)} %param.15) | copy-start | bytes 124
  88.9 20.6 %collective-permute-start.4 = (bf16[2048,128]{1,0:T(8,128)(2,1)}, bf16[2048,128]{1,0:T(8,128)(2,1)S(1)}, u32[]{:S(2)}, u32[]{:S(2)}) collective-permute-start(bf16[2048,128]{1,0:T(8,128)(2,1)} %bitcast.5), channel_id=1, source_target_pairs={{0,64},{64,128},{128,192},{192,0},{1,65},{65,129},{129,193},{193,1... | collective-permute-start | bytes 1572872 | tf_op jit(solution)/shard_map/ppermute | solution.py:428
  89.3 20.8 %collective-permute-start.5 = (bf16[2048,128]{1,0:T(8,128)(2,1)S(1)}, bf16[2048,128]{1,0:T(8,128)(2,1)S(1)}, u32[]{:S(2)}, u32[]{:S(2)}) collective-permute-start(bf16[2048,128]{1,0:T(8,128)(2,1)S(1)} %bitcast.22), channel_id=1, source_target_pairs={{0,192},{64,0},{128,64},{192,128},{1,193},{65,1},{129,65},{193,129... | collective-permute-start | bytes 1572872 | tf_op jit(solution)/shard_map/ppermute | solution.py:429
  98.2 27.2 %collective-permute-start.1 = (bf16[2048,128]{1,0:T(8,128)(2,1)S(1)}, bf16[2048,128]{1,0:T(8,128)(2,1)S(1)}, u32[]{:S(2)}, u32[]{:S(2)}) collective-permute-start(bf16[2048,128]{1,0:T(8,128)(2,1)S(1)} %collective-permute-done.below_a), channel_id=1, source_target_pairs={{0,64},{64,128},{128,192},{192,0},{1,65},{65,129},{129,193},{193,1... | collective-permute-start | bytes 1572872 | tf_op jit(solution)/shard_map/ppermute | solution.py:430
  98.9 27.4 %collective-permute-start.3 = (bf16[2048,128]{1,0:T(8,128)(2,1)S(1)}, bf16[2048,128]{1,0:T(8,128)(2,1)}, u32[]{:S(2)}, u32[]{:S(2)}) collective-permute-start(bf16[2048,128]{1,0:T(8,128)(2,1)S(1)} %collective-permute-done.2.above_b), channel_id=1, source_target_pairs={{0,192},{64,0},{128,64},{192,128},{1,193},{65,1},{129,65},{193,129... | collective-permute-start | bytes 1572872 | tf_op jit(solution)/shard_map/ppermute | solution.py:431
  103.7 1.0 copy-start.7
  104.7 18.9 %copy-start.6 = (bf16[768,736]{1,0:T(8,128)(2,1)}, bf16[768,736]{1,0:T(8,128)(2,1)S(1)}, u32[]{:S(2)}) copy-start(bf16[768,736]{1,0:T(8,128)(2,1)S(1)} %get-tuple-element.21.table_ref) | copy-start | bytes 3391492
  123.6 1.8 copy-start.3
  125.4 0.9 copy-start.11
  150.7 57.0 %copy-start.1 = (bf16[6,640,384]{2,1,0:T(8,128)(2,1)S(1)}, bf16[6,640,384]{2,1,0:T(8,128)(2,1)}, u32[]{:S(2)}) copy-start(bf16[6,640,384]{2,1,0:T(8,128)(2,1)} %basis_ref.3) | copy-start | bytes 8847364

commit v2 on v1

--- a/solution.py
+++ b/solution.py
@@ -77,7 +77,7 @@
 def to_degrees(lat_basis, rows):
     slots, lats, degrees = lat_basis.shape
     features = rows.shape[1]
-    together = 2 if slots % 2 == 0 else 1
+    together = 3 if slots % 3 == 0 else 1
     return pl.pallas_call(
         degrees_kernel,
         grid=(slots // together,),

time: 211 us -> 211 us (level)
  no operation moved by 1% of the time
where the time goes in v2:
time: 211 us; the launch traced here: 210 us
  blocking collectives  93.9 us (45%)
  Pallas kernels  48.7 us (23%)
  starting transfers between devices  27.8 us (13%)
  waiting for transfers between devices  14.4 us (7%)
  other arithmetic  13.7 us (6%)
  local copies, waits for them, and re-layouts  11.5 us (5%)
    all_to_all x2, blocking collectives, exchange(): lax.all_to_all(chunks, 'band', split_axis=0, concat_axis=0, tiled=True)  93.9 us
    pallas_call x1, Pallas kernels, column_spectrum(): pl.pallas_call(functools.partial(columns_kernel, sources), grid=(lats //...  22.4 us
    all_to_all x2, starting transfers between devices, exchange(): lax.all_to_all(chunks, 'band', split_axis=0, concat_axis=0, tiled=True)  18 us
    pallas_call x1, Pallas kernels, place_near(): pl.pallas_call(functools.partial(near_kernel, padded), in_specs=[pl.Block...  13.5 us
    unnamed x27, local copies, waits for them, and re-layouts  8.84 us
    sort x1, other arithmetic, requests(): keys, order = lax.sort((keys, columns), num_keys=1)  7.19 us
    ppermute x1, waiting for transfers between devices, gathered_over_members(): below_a = lax.ppermute(first, 'ens', up)  6.03 us
    pallas_call x1, Pallas kernels, fetch_rows(): pl.pallas_call(fetch_kernel, in_specs=[pl.BlockSpec(memory_space=pltpu.SM...  5.18 us
  transfers between devices with their start and end apart: 8, of which 6 were waited for; matrix products, arithmetic and copies ran while one was open for 3% of the time, Pallas kernels for 9%

profile of v2, /device:TPU:2, one launch (start us, length us, event | category | flops | bytes accessed | tf_op | source)
XLA Modules:
  0.0 210.3 jit_solution(14306000286249914140)
XLA Ops:
  0.0 1.0 multiply_add_fusion
  1.0 0.1 reshape.103
  1.1 7.2 %sort.15 = (s32[14400]{0:T(1024)S(1)}, s32[14400]{0:T(1024)S(1)}) sort(s32[14400]{0:T(1024)S(1)} %reshape.103, s32[14400]{0:T(1024)S(1)} %iota.35), dimensions={0}, to_apply=%region_0.0 | sort | flops 201600 | bytes 230400 | tf_op jit(solution)/shard_map/sort | solution.py:446
  8.3 0.2 reshape.107
  8.5 0.1 broadcast_subtract_fusion
  8.5 0.1 pad_dynamic-slice_fusion.2
  8.6 0.6 pad.13
  9.2 12.0 %all-to-all-start = ((s32[64,1,64]{2,1,0:T(1,128)}), s32[64,1,64]{2,1,0:T(1,128)S(1)}, u32[]{:S(2)}, u32[]{:S(2)}) async-start(s32[64,1,64]{2,1,0:T(1,128)} %bitcast.2), calls=%async_computation | async-start | bytes 65536 | tf_op jit(solution)/shard_map/all_to_all | solution.py:340
  21.3 0.0 copy-start
  21.3 1.8 copy-done
  23.1 1.3 copy-done.4
  24.4 3.5 %to_latitudes.1 = bf16[7680,128]{1,0:T(8,128)(2,1)} custom-call(bf16[6,640,384]{2,1,0:T(8,128)(2,1)S(1)} %copy-done, bf16[6,384,256]{2,1,0:T(8,128)(2,1)S(1)} %copy-done.4), custom_call_target="tpu_custom_call" | custom-call | flops 754974720 | bytes 6094848 | tf_op jit(solution)/shard_map/to_latitudes/pallas_call | solution.py:36
  27.8 2.0 all-to-all-done.ids_ref
  29.8 2.0 copy-done.2
  31.9 5.2 %fetch_rows.1 = bf16[4096,128]{1,0:T(8,128)(2,1)S(1)} custom-call(s32[64,1,64]{2,1,0:T(1,128)S(1)} %all-to-all-done.ids_ref, bf16[14400,128]{1,0:T(8,128)(2,1)S(1)} %copy-done.2), custom_call_target="tpu_custom_call" | custom-call | bytes 94699520 | tf_op jit(solution)/shard_map/fetch_rows/pallas_call | solution.py:360
  37.1 36.9 %all_to_all.20 = bf16[64,64,128]{2,1,0:T(8,128)(2,1)S(1)} all-to-all(bf16[64,64,128]{2,1,0:T(8,128)(2,1)S(1)} %bitcast.16), channel_id=1, replica_groups=mesh['ens'=4,'band'=64] {'band'}, dimensions={0} | all-to-all | bytes 2097152 | tf_op jit(solution)/shard_map/all_to_all | solution.py:340
  74.0 6.0 %all-to-all-start.2 = ((bf16[64,120,128]{2,1,0:T(8,128)(2,1)}), bf16[64,120,128]{2,1,0:T(8,128)(2,1)}, u32[]{:S(2)}, u32[]{:S(2)}) async-start(bf16[64,120,128]{2,1,0:T(8,128)(2,1)} %bitcast.6), calls=%async_computation.2 | async-start | bytes 3932160 | tf_op jit(solution)/shard_map/all_to_all | solution.py:340
  79.9 0.0 copy-done.10
  80.0 0.1 reshape.112
  80.1 0.1 copy.17
  80.2 0.1 reshape.113
  80.3 0.1 fusion.22
  80.3 0.2 reshape.104
  80.5 0.1 reshape.105
  80.7 0.1 fusion.7
  80.9 0.1 fusion.23
  81.0 0.4 fusion.12
  81.4 0.9 fusion.31
  82.3 1.6 collective-permute-start
  83.8 1.7 collective-permute-start.2
  85.5 0.2 copy.18
  85.7 0.0 copy-start.5
  85.7 0.0 copy-start.8
  85.7 0.0 copy-start.9
  85.7 0.0 copy-start.12
  85.8 1.7 fusion.4
  87.4 1.4 multiply_sine_fusion
  88.9 0.4 collective-permute-start.4
  89.3 2.9 %collective-permute-start.5 = (bf16[2048,128]{1,0:T(8,128)(2,1)S(1)}, bf16[2048,128]{1,0:T(8,128)(2,1)S(1)}, u32[]{:S(2)}, u32[]{:S(2)}) collective-permute-start(bf16[2048,128]{1,0:T(8,128)(2,1)S(1)} %bitcast.22), channel_id=1, source_target_pairs={{0,192},{64,0},{128,64},{192,128},{1,193},{65,1},{129,65},{193,129... | collective-permute-start | bytes 1572872 | tf_op jit(solution)/shard_map/ppermute | solution.py:429
  92.2 6.0 %collective-permute-done.below_a = bf16[2048,128]{1,0:T(8,128)(2,1)S(1)} collective-permute-done((bf16[2048,128]{1,0:T(8,128)(2,1)S(1)}, bf16[2048,128]{1,0:T(8,128)(2,1)S(1)}, u32[]{:S(2)}, u32[]{:S(2)}) %collective-permute-start) | collective-permute-done | bytes 524320 | tf_op jit(solution)/shard_map/ppermute | solution.py:426
  98.2 0.4 collective-permute-start.1
  98.6 0.2 collective-permute-done.2.above_b
  98.9 2.9 %collective-permute-start.3 = (bf16[2048,128]{1,0:T(8,128)(2,1)S(1)}, bf16[2048,128]{1,0:T(8,128)(2,1)}, u32[]{:S(2)}, u32[]{:S(2)}) collective-permute-start(bf16[2048,128]{1,0:T(8,128)(2,1)S(1)} %collective-permute-done.2.above_b), channel_id=1, source_target_pairs={{0,192},{64,0},{128,64},{192,128},{1,193},{65,1},{129,65},{193,129... | collective-permute-start | bytes 1572872 | tf_op jit(solution)/shard_map/ppermute | solution.py:431
  101.7 0.4 fusion.19
  102.1 1.6 fourier_tables.1
  103.7 0.0 copy-start.7
  103.7 1.0 copy-done.7
  104.7 0.0 copy-done.8
  104.7 0.7 pad_maximum_fusion.first_ref
  105.4 0.0 copy-done.12
  105.4 0.6 broadcast_multiply_fusion.weight_ref
  106.0 3.5 %collective-permute-done.4.below_b = bf16[2048,128]{1,0:T(8,128)(2,1)S(1)} collective-permute-done((bf16[2048,128]{1,0:T(8,128)(2,1)}, bf16[2048,128]{1,0:T(8,128)(2,1)S(1)}, u32[]{:S(2)}, u32[]{:S(2)}) %collective-permute-start.4) | collective-permute-done | bytes 524320 | tf_op jit(solution)/shard_map/ppermute | solution.py:428
  109.5 0.6 collective-permute-done.5.above_a
  110.1 13.5 %place_near.1.near_ref = bf16[14400,128]{1,0:T(8,128)(2,1)S(1)} custom-call(s32[256,57]{1,0:T(8,128)S(1)} %bitcast.17, bf16[4096,128]{1,0:T(8,128)(2,1)S(1)} %bitcast.14, bf16[2048,128]{1,0:T(8,128)(2,1)S(1)} %collective-permute-done.5.above_a, bf16[2048,128]{1,0:T(8,128)(2,1)S(1)} %collective-permute-done.2.above_b, ...), custom_call_target="tpu_custom_call" | custom-call | bytes 31457280 | tf_op jit(solution)/shard_map/place_near/pallas_call | solution.py:404
  123.6 0.0 copy-done.6
  123.6 0.0 copy-start.3
  123.6 1.8 copy-done.3
  125.4 0.0 collective-permute-done.1.far_first_ref
  125.4 0.9 copy-done.11
  126.3 0.0 collective-permute-done.3.far_second_ref
  126.3 2.1 all-to-all-done.2
  128.3 22.4 %column_spectrum.1 = bf16[7680,128]{1,0:T(8,128)(2,1)} custom-call(f32[10]{0:T(128)} %broadcast_multiply_fusion.weight_ref, s32[256,57]{1,0:T(8,128)} %bitcast.18, bf16[2048,128]{1,0:T(8,128)(2,1)} %copy-done.11, bf16[2048,128]{1,0:T(8,128)(2,1)} %collective-permute-done.3.far_second_ref, bf16[7680,128]{1,0:T(8,128)(2,1)} %bitcast.7.rows_ref, ...), custom_call_target="tpu_custom_call" | custom-call | flops 7549747200 | bytes 9879552 | tf_op jit(solution)/shard_map/column_spectrum/pallas_call | solution.py:287
  150.7 57.0 %all_to_all.21 = bf16[64,120,128]{2,1,0:T(8,128)(2,1)S(1)} all-to-all(bf16[64,120,128]{2,1,0:T(8,128)(2,1)} %bitcast.19), channel_id=1, replica_groups=mesh['ens'=4,'band'=64] {'band'}, dimensions={0} | all-to-all | bytes 3932160 | tf_op jit(solution)/shard_map/all_to_all | solution.py:340
  207.7 2.6 %to_degrees.1 = f32[6,384,256]{2,1,0:T(8,128)} custom-call(bf16[6,640,384]{2,1,0:T(8,128)(2,1)S(1)} %copy-done.1, bf16[7680,128]{1,0:T(8,128)(2,1)S(1)} %bitcast.15), custom_call_target="tpu_custom_call" | custom-call | flops 754974720 | bytes 7274496 | tf_op jit(solution)/shard_map/to_degrees/pallas_call | solution.py:81
  (20 shorter events, 0.1 us)
Async XLA Ops:
  9.2 20.6 %all-to-all-start = ((s32[64,1,64]{2,1,0:T(1,128)}), s32[64,1,64]{2,1,0:T(1,128)S(1)}, u32[]{:S(2)}, u32[]{:S(2)}) async-start(s32[64,1,64]{2,1,0:T(1,128)} %bitcast.2), calls=%async_computation | async-start | bytes 65536 | tf_op jit(solution)/shard_map/all_to_all | solution.py:340
  21.3 1.8 copy-start
  23.1 1.3 copy-start.4
  29.8 2.0 copy-start.2
  74.0 6.0 %copy-start.10 = (s32[384]{0:T(512)S(1)}, s32[384]{0:T(512)}, u32[]{:S(2)}) copy-start(s32[384]{0:T(512)} %param.16) | copy-start | bytes 4612
  74.0 54.4 %all-to-all-start.2 = ((bf16[64,120,128]{2,1,0:T(8,128)(2,1)}), bf16[64,120,128]{2,1,0:T(8,128)(2,1)}, u32[]{:S(2)}, u32[]{:S(2)}) async-start(bf16[64,120,128]{2,1,0:T(8,128)(2,1)} %bitcast.6), calls=%async_computation.2 | async-start | bytes 3932160 | tf_op jit(solution)/shard_map/all_to_all | solution.py:340
  82.3 16.0 %collective-permute-start = (bf16[2048,128]{1,0:T(8,128)(2,1)S(1)}, bf16[2048,128]{1,0:T(8,128)(2,1)S(1)}, u32[]{:S(2)}, u32[]{:S(2)}) collective-permute-start(bf16[2048,128]{1,0:T(8,128)(2,1)S(1)} %bitcast.21), channel_id=1, source_target_pairs={{0,64},{64,128},{128,192},{192,0},{1,65},{65,129},{129,193},{193,1... | collective-permute-start | bytes 1572872 | tf_op jit(solution)/shard_map/ppermute | solution.py:426
  83.8 15.0 %collective-permute-start.2 = (bf16[2048,128]{1,0:T(8,128)(2,1)}, bf16[2048,128]{1,0:T(8,128)(2,1)S(1)}, u32[]{:S(2)}, u32[]{:S(2)}) collective-permute-start(bf16[2048,128]{1,0:T(8,128)(2,1)} %bitcast.5), channel_id=1, source_target_pairs={{0,192},{64,0},{128,64},{192,128},{1,193},{65,1},{129,65},{193,129... | collective-permute-start | bytes 1572872 | tf_op jit(solution)/shard_map/ppermute | solution.py:427
  85.7 24.4 %copy-start.5 = (s32[4,64,57]{2,1,0:T(8,128)}, s32[4,64,57]{2,1,0:T(8,128)S(1)}, u32[]{:S(2)}) copy-start(s32[4,64,57]{2,1,0:T(8,128)S(1)} %copy.16) | copy-start | bytes 175108
  85.7 19.0 %copy-start.8 = (bf16[128,256]{1,0:T(8,128)(2,1)S(1)}, bf16[128,256]{1,0:T(8,128)(2,1)}, u32[]{:S(2)}) copy-start(bf16[128,256]{1,0:T(8,128)(2,1)} %param.21) | copy-start | bytes 196612
  85.7 19.0 %copy-start.9 = (bf16[128,256]{1,0:T(8,128)(2,1)S(1)}, bf16[128,256]{1,0:T(8,128)(2,1)}, u32[]{:S(2)}) copy-start(bf16[128,256]{1,0:T(8,128)(2,1)} %param.20) | copy-start | bytes 196612
  85.7 19.7 %copy-start.12 = (f32[10]{0:T(128)S(1)}, f32[10]{0:T(128)}, u32[]{:S(2)}) copy-start(f32[10]{0:T(128)} %param.15) | copy-start | bytes 124
  88.9 20.6 %collective-permute-start.4 = (bf16[2048,128]{1,0:T(8,128)(2,1)}, bf16[2048,128]{1,0:T(8,128)(2,1)S(1)}, u32[]{:S(2)}, u32[]{:S(2)}) collective-permute-start(bf16[2048,128]{1,0:T(8,128)(2,1)} %bitcast.5), channel_id=1, source_target_pairs={{0,64},{64,128},{128,192},{192,0},{1,65},{65,129},{129,193},{193,1... | collective-permute-start | bytes 1572872 | tf_op jit(solution)/shard_map/ppermute | solution.py:428
  89.3 20.8 %collective-permute-start.5 = (bf16[2048,128]{1,0:T(8,128)(2,1)S(1)}, bf16[2048,128]{1,0:T(8,128)(2,1)S(1)}, u32[]{:S(2)}, u32[]{:S(2)}) collective-permute-start(bf16[2048,128]{1,0:T(8,128)(2,1)S(1)} %bitcast.22), channel_id=1, source_target_pairs={{0,192},{64,0},{128,64},{192,128},{1,193},{65,1},{129,65},{193,129... | collective-permute-start | bytes 1572872 | tf_op jit(solution)/shard_map/ppermute | solution.py:429
  98.2 27.2 %collective-permute-start.1 = (bf16[2048,128]{1,0:T(8,128)(2,1)S(1)}, bf16[2048,128]{1,0:T(8,128)(2,1)S(1)}, u32[]{:S(2)}, u32[]{:S(2)}) collective-permute-start(bf16[2048,128]{1,0:T(8,128)(2,1)S(1)} %collective-permute-done.below_a), channel_id=1, source_target_pairs={{0,64},{64,128},{128,192},{192,0},{1,65},{65,129},{129,193},{193,1... | collective-permute-start | bytes 1572872 | tf_op jit(solution)/shard_map/ppermute | solution.py:430
  98.9 27.4 %collective-permute-start.3 = (bf16[2048,128]{1,0:T(8,128)(2,1)S(1)}, bf16[2048,128]{1,0:T(8,128)(2,1)}, u32[]{:S(2)}, u32[]{:S(2)}) collective-permute-start(bf16[2048,128]{1,0:T(8,128)(2,1)S(1)} %collective-permute-done.2.above_b), channel_id=1, source_target_pairs={{0,192},{64,0},{128,64},{192,128},{1,193},{65,1},{129,65},{193,129... | collective-permute-start | bytes 1572872 | tf_op jit(solution)/shard_map/ppermute | solution.py:431
  103.7 1.0 copy-start.7
  104.7 18.9 %copy-start.6 = (bf16[768,736]{1,0:T(8,128)(2,1)}, bf16[768,736]{1,0:T(8,128)(2,1)S(1)}, u32[]{:S(2)}) copy-start(bf16[768,736]{1,0:T(8,128)(2,1)S(1)} %get-tuple-element.21.table_ref) | copy-start | bytes 3391492
  123.6 1.8 copy-start.3
  125.4 0.9 copy-start.11
  150.7 57.0 %copy-start.1 = (bf16[6,640,384]{2,1,0:T(8,128)(2,1)S(1)}, bf16[6,640,384]{2,1,0:T(8,128)(2,1)}, u32[]{:S(2)}) copy-start(bf16[6,640,384]{2,1,0:T(8,128)(2,1)} %basis_ref.3) | copy-start | bytes 8847364
